TPU v7x, 32 devices: a whole 2x2x4 slice. The times are simulated.
32 devices in a mesh: parts: 2 (over y), row: 16 (over z, x, core).
Axes of the slice: x: 2, y: 2, z: 4, core: 2. Of those that a mesh axis runs over, the one named last changes fastest.
Arguments:
- node_latent: bfloat16 [32768, 256], P(('parts', 'row')), parts along dimension 0, may hold values from -120 to 120
- agg_saved: bfloat16 [32768, 256], P(('parts', 'row')), parts along dimension 0, may hold values from -12 to 12
- node_cot: bfloat16 [32768, 256], P(('parts', 'row')), parts along dimension 0, may hold values from -6 to 6
- edge_latent: bfloat16 [24576, 256], P(('parts', 'row')), parts along dimension 0, may hold values from -120 to 120
- edge_cot: bfloat16 [24576, 256], P(('parts', 'row')), parts along dimension 0, may hold values from -6 to 6
- send_local: int32 [192, 128], P(('parts', 'row')), parts along dimension 0, may hold values from 0 to 1023
- recv_local: int32 [192, 128], P(('parts', 'row')), parts along dimension 0, may hold values from 0 to 1023
- send_slot: int32 [192], P(('parts', 'row')), parts along dimension 0, may hold values from 0 to 2, as said below
- recv_slot: int32 [192], P(('parts', 'row')), parts along dimension 0, may hold values from 0 to 2, as said below
- tile_count: int32 [32], P(('parts', 'row')), parts along dimension 0, may hold values from 3 to 6, as said below
- edge_w_in: bfloat16 [768, 256], replicated, may hold values from -0.21875 to 0.21875
- edge_w_out: bfloat16 [256, 256], replicated, may hold values from -0.375 to 0.375
- edge_gain: float32 [256], replicated, may hold values from 0.1 to 1.9
- node_w_in: bfloat16 [512, 256], replicated, may hold values from -0.25 to 0.25
- node_w_out: bfloat16 [256, 256], replicated, may hold values from -0.375 to 0.375
- node_gain: float32 [256], replicated, may hold values from 0.1 to 1.9
Outputs:
- node_grad: bfloat16 [32768, 256], P(('parts', 'row')), parts along dimension 0
- edge_grad: bfloat16 [24576, 256], P(('parts', 'row')), parts along dimension 0
- edge_grad_w_in: float32 [1536, 256], P('parts'), parts along dimension 0
- edge_grad_w_out: float32 [512, 256], P('parts'), parts along dimension 0
- edge_grad_gain: float32 [512], P('parts'), parts along dimension 0
- node_grad_w_in: float32 [1024, 256], P('parts'), parts along dimension 0
- node_grad_w_out: float32 [512, 256], P('parts'), parts along dimension 0
- node_grad_gain: float32 [512], P('parts'), parts along dimension 0
There are 2 independent parts, one for each index of `parts`. A program takes and returns all parts, laid end to end along the dimension named above; an argument that names none is the same for every part. Nothing has to cross between parts.
Inputs may be any that keep to these rules, and one draw needn't show every extreme that they name: Tiles 0 to tile_count - 1 of a device hold edges, its other tile slots are padding; some device has all 6 live. `send_slot`: on every device, the first 3 tiles name each sender block once. `recv_slot`: on every device, the first 3 tiles name each receiver block once.
All inputs are finite; a program needn't handle non-finite values.
Results may differ from a plain program's by a relative error of at most 0.0056.
Values may be sent and summed in bfloat16 or wider, within the bound.
A program may use at most 128 MiB of HBM per device.

v0:
```python
import jax
import jax.numpy as jnp
from jax import lax
from jax.sharding import PartitionSpec as P

EPSILON = 1e-05


def passed_along(block, axis, distance):
    devices = range(lax.axis_size(axis))
    route = [((i - distance) % len(devices), i) for i in devices]
    return lax.ppermute(block, axis, route)


def mlp_backward(inputs, w_in, w_out, norm_gain, cotangent):
    preact = jnp.dot(inputs, w_in, preferred_element_type=jnp.float32)
    activation = jax.nn.silu(preact).astype(jnp.bfloat16)
    output = jnp.dot(activation, w_out, preferred_element_type=jnp.float32)
    row_mean = jnp.mean(output, axis=-1, keepdims=True)
    centred = output - row_mean
    inverse = lax.rsqrt(jnp.mean(centred * centred, axis=-1, keepdims=True) + EPSILON)
    normed = centred * inverse
    grad_gain = jnp.sum(cotangent * normed, axis=0)
    scaled = cotangent * norm_gain
    out_grad = inverse * (
        scaled
        - jnp.mean(scaled, axis=-1, keepdims=True)
        - normed * jnp.mean(scaled * normed, axis=-1, keepdims=True)
    )
    out_grad = out_grad.astype(jnp.bfloat16)
    grad_w_out = jnp.dot(activation.T, out_grad, preferred_element_type=jnp.float32)
    sigmoid_pre = jax.nn.sigmoid(preact)
    act_grad = jnp.dot(out_grad, w_out.T, preferred_element_type=jnp.float32)
    pre_grad = (act_grad * sigmoid_pre * (1.0 + preact * (1.0 - sigmoid_pre))).astype(jnp.bfloat16)
    grad_w_in = jnp.dot(inputs.T, pre_grad, preferred_element_type=jnp.float32)
    in_grad = jnp.dot(pre_grad, w_in.T, preferred_element_type=jnp.float32)
    return (in_grad, grad_w_in, grad_w_out, grad_gain)


def on_device(
    node_latent,
    agg_saved,
    node_cot,
    edge_latent,
    edge_cot,
    send_local,
    recv_local,
    send_slot,
    recv_slot,
    tile_count,
    edge_w_in,
    edge_w_out,
    edge_gain,
    node_w_in,
    node_w_out,
    node_gain,
):
    features = node_latent.shape[1]
    block_rows = node_latent.shape[0]
    devices = lax.axis_size("row")
    stride = devices // 8
    tile_total, tile_width = send_local.shape
    node_scale = (block_rows * devices) ** (-0.5)
    edge_scale = (tile_total * tile_width * devices) ** (-0.5)
    node_in = jnp.concatenate([node_latent, agg_saved], axis=1)
    node_cotangent = node_cot.astype(jnp.float32)
    node_in_grad, node_gw_in, node_gw_out, node_g_gain = mlp_backward(
        node_in, node_w_in, node_w_out, node_gain, node_cotangent
    )
    agg_grad = node_in_grad[:, features:].astype(jnp.bfloat16)
    paired = jnp.stack([node_latent, agg_grad])
    recv_tables = [paired]
    for offset in (1, 2):
        recv_tables.append(passed_along(paired, "row", -offset))
    send_tables = [node_latent]
    for offset in (1, 2):
        send_tables.append(passed_along(node_latent, "row", -offset * stride))
    recv_stack = jnp.stack(recv_tables)
    recv_latent = recv_stack[:, 0].reshape(3 * block_rows, features)
    recv_agg = recv_stack[:, 1].reshape(3 * block_rows, features)
    send_latent = jnp.concatenate(send_tables, axis=0)
    recv_index = (recv_slot[:, None] * block_rows + recv_local).reshape(-1)
    send_index = (send_slot[:, None] * block_rows + send_local).reshape(-1)
    live_tiles = (jnp.arange(tile_total, dtype=jnp.int32) < tile_count[0]).astype(jnp.float32)
    live_edges = jnp.repeat(live_tiles, tile_width)[:, None]
    edge_in = jnp.concatenate(
        [
            edge_latent,
            jnp.take(send_latent, send_index, axis=0),
            jnp.take(recv_latent, recv_index, axis=0),
        ],
        axis=1,
    )
    edge_cotangent = live_edges * (
        edge_cot.astype(jnp.float32) + jnp.take(recv_agg, recv_index, axis=0).astype(jnp.float32)
    )
    edge_in_grad, edge_gw_in, edge_gw_out, edge_g_gain = mlp_backward(
        edge_in, edge_w_in, edge_w_out, edge_gain, edge_cotangent
    )
    sender_grad = (
        edge_in_grad[:, features : 2 * features]
        .astype(jnp.bfloat16)
        .reshape(tile_total, tile_width, features)
    )
    receiver_grad = (
        edge_in_grad[:, 2 * features :]
        .astype(jnp.bfloat16)
        .reshape(tile_total, tile_width, features)
    )
    node_ids = jnp.arange(block_rows, dtype=jnp.int32)[:, None]

    def add_block(accum, start_row, local_rows, grads):
        selector = (node_ids == local_rows[None, :]).astype(jnp.bfloat16)
        tile_term = jnp.dot(selector, grads, preferred_element_type=jnp.float32)
        current = lax.dynamic_slice_in_dim(accum, start_row, block_rows, 0)
        return lax.dynamic_update_slice_in_dim(accum, current + tile_term, start_row, 0)

    def add_tile(carried, pieces):
        send_acc, recv_acc = carried
        slot_s, local_s, grad_s, slot_r, local_r, grad_r = pieces
        send_acc = add_block(send_acc, slot_s * block_rows, local_s, grad_s)
        recv_acc = add_block(recv_acc, slot_r * block_rows, local_r, grad_r)
        return ((send_acc, recv_acc), None)

    empty_sums = jnp.zeros((3 * block_rows, features), jnp.float32)
    (send_acc, recv_acc), unused = lax.scan(
        add_tile,
        (empty_sums, empty_sums),
        (send_slot, send_local, sender_grad, recv_slot, recv_local, receiver_grad),
    )
    send_parts = send_acc.reshape(3, block_rows, features)
    recv_parts = recv_acc.reshape(3, block_rows, features)
    recv_total = recv_parts[0]
    send_total = send_parts[0]
    for offset in (1, 2):
        recv_total = recv_total + passed_along(
            recv_parts[offset].astype(jnp.bfloat16), "row", offset
        ).astype(jnp.float32)
        send_total = send_total + passed_along(
            send_parts[offset].astype(jnp.bfloat16), "row", offset * stride
        ).astype(jnp.float32)
    node_grad = (node_cotangent + node_in_grad[:, :features] + recv_total + send_total).astype(
        jnp.bfloat16
    )
    edge_grad = (edge_cotangent + edge_in_grad[:, :features]).astype(jnp.bfloat16)
    edge_gw_in, edge_gw_out, edge_g_gain, node_gw_in, node_gw_out, node_g_gain = lax.psum(
        (edge_gw_in, edge_gw_out, edge_g_gain, node_gw_in, node_gw_out, node_g_gain), "row"
    )
    return (
        node_grad,
        edge_grad,
        edge_gw_in * edge_scale,
        edge_gw_out * edge_scale,
        edge_g_gain * edge_scale,
        node_gw_in * node_scale,
        node_gw_out * node_scale,
        node_g_gain * node_scale,
    )


def solution(mesh):
    placed = (
        P(("parts", "row"), None),
        P(("parts", "row"), None),
        P(("parts", "row"), None),
        P(("parts", "row"), None),
        P(("parts", "row"), None),
        P(("parts", "row"), None),
        P(("parts", "row"), None),
        P(("parts", "row")),
        P(("parts", "row")),
        P(("parts", "row")),
        P(),
        P(),
        P(),
        P(),
        P(),
        P(),
    )
    return jax.shard_map(
        on_device,
        mesh=mesh,
        in_specs=placed,
        out_specs=(
            P(("parts", "row"), None),
            P(("parts", "row"), None),
            P("parts", None),
            P("parts", None),
            P("parts"),
            P("parts", None),
            P("parts", None),
            P("parts"),
        ),
        check_vma=False,
    )
```

profile of v0, /device:TPU:0, one launch (start us, length us, event | category | flops | bytes accessed | tf_op | source)
XLA Modules:
  0.0 300.2 jit_solution(16034324460617562049)
XLA Ops:
  7.2 1.1 constant_dynamic-update-slice_fusion.3
  8.4 1.1 constant_dynamic-update-slice_fusion.2
  9.5 2.7 multiply_convert_fusion
  13.6 0.9 fusion.26
  15.6 0.8 copy-done.13
  17.4 1.1 fusion.32
  18.5 5.4 %collective-permute-start.2 = (bf16[2,1024,256]{2,1,0:T(8,128)(2,1)}, bf16[2,1024,256]{2,1,0:T(8,128)(2,1)}, u32[]{:S(2)}, u32[]{:S(2)}) collective-permute-start(bf16[2,1024,256]{2,1,0:T(8,128)(2,1)} %get-tuple-element.172), channel_id=1, source_target_pairs={{1,0},{2,1},{3,2},{4,3},{5,4},{6,5},{7,6},{8,7},{9,8},{10,9},{11,1... | collective-permute-start | bytes 3145736 | tf_op jit(solution)/shard_map/ppermute | solution.py:12
  24.5 1.3 collective-permute-start
  26.3 1.1 fusion.43
  28.9 2.0 copy.37
  30.9 1.3 copy.52
  32.8 2.6 fusion.42
  35.4 40.4 %collective-permute-done = bf16[1024,256]{1,0:T(8,128)(2,1)} collective-permute-done((bf16[1024,256]{1,0:T(8,128)(2,1)S(1)}, bf16[1024,256]{1,0:T(8,128)(2,1)}, u32[]{:S(2)}, u32[]{:S(2)}) %collective-permute-start) | collective-permute-done | bytes 524320 | tf_op jit(solution)/shard_map/ppermute | solution.py:12
  75.8 5.6 %collective-permute-done.1 = bf16[1024,256]{1,0:T(8,128)(2,1)} collective-permute-done((bf16[1024,256]{1,0:T(8,128)(2,1)S(1)}, bf16[1024,256]{1,0:T(8,128)(2,1)}, u32[]{:S(2)}, u32[]{:S(2)}) %collective-permute-start.1) | collective-permute-done | bytes 524320 | tf_op jit(solution)/shard_map/ppermute | solution.py:12
  81.4 1.3 pad_maximum_fusion.1
  82.7 2.7 gather_fusion
  85.4 0.9 broadcast_select_fusion.1
  86.3 1.9 pad_maximum_fusion
  88.4 3.3 %gather_fusion.1 = bf16[768,256]{1,0:T(8,128)(2,1)} fusion(bf16[3072,256]{1,0:T(8,128)(2,1)S(1)} %bitcast.68, s32[1024]{0:T(1024)S(1)} %pad_clamp_fusion), kind=kCustom, calls=%fused_computation.1.clone | custom fusion | bytes 789504 | tf_op jit(solution)/shard_map/jit(_take)/gather | solution.py:90
  91.7 1.2 broadcast_select_fusion
  92.9 2.6 multiply_convert_fusion.2
  96.0 3.3 %gather_fusion.2 = bf16[768,256]{1,0:T(8,128)(2,1)} fusion(bf16[3072,256]{1,0:T(8,128)(2,1)S(1)} %bitcast.67, s32[1024]{0:T(1024)S(1)} %pad_clamp_fusion), kind=kCustom, calls=%fused_computation.2.clone | custom fusion | bytes 789504 | tf_op jit(solution)/shard_map/jit(_take)/gather | solution.py:95
  99.3 1.2 copy.38
  100.5 1.8 multiply_reduce_fusion.1
  102.7 1.0 fusion.41
  105.0 1.5 fusion.28
  107.0 1.1 copy.53
  108.2 2.0 broadcast_in_dim.10.clone
  110.2 2.1 broadcast_in_dim.10.clone2
  112.3 61.8 %while.14 = (s32[]{:T(128)}, f32[3072,256]{0,1:T(8,128)}, f32[3072,256]{0,1:T(8,128)}, s32[6]{0:T(128)S(1)}, s32[6,128]{1,0:T(8,128)}, /*index=5*/bf16[6,128,256...) while((s32[]{:T(128)}, f32[3072,256]{0,1:T(8,128)}, ...), condition=%wide.region_9.11_spmd.clone.clone, body=%wide.region_8.10_spmd.clone.clone.sunk | while | flops 135004160 | bytes 24251852 | solution.py:126
  112.3 0.7 dynamic_slice.74
  113.7 1.3 constant_dynamic-slice_fusion.7
  118.0 1.3 constant_dynamic-slice_fusion.6
  121.0 1.5 constant_dynamic-update-slice_fusion.5
  124.0 1.3 constant_dynamic-slice_fusion.7
  128.3 1.3 constant_dynamic-slice_fusion.6
  131.3 1.5 constant_dynamic-update-slice_fusion.5
  134.2 1.3 constant_dynamic-slice_fusion.7
  138.6 1.3 constant_dynamic-slice_fusion.6
  141.6 1.5 constant_dynamic-update-slice_fusion.5
  144.5 1.3 constant_dynamic-slice_fusion.7
  148.9 1.3 constant_dynamic-slice_fusion.6
  151.9 1.5 constant_dynamic-update-slice_fusion.5
  154.8 1.3 constant_dynamic-slice_fusion.7
  159.1 1.3 constant_dynamic-slice_fusion.6
  162.2 1.5 constant_dynamic-update-slice_fusion.5
  165.1 1.3 constant_dynamic-slice_fusion.7
  169.4 1.3 constant_dynamic-slice_fusion.6
  172.5 1.6 constant_dynamic-update-slice_fusion.5
  174.0 2.2 convert.17
  176.3 1.0 fusion.34
  177.6 1.0 fusion.35
  178.6 2.0 collective-permute-start.6
  180.6 1.5 collective-permute-start.7
  182.2 2.2 add_convert_fusion
  184.4 1.9 copy.45
  186.3 72.7 %all-reduce = (f32[256]{0:T(256)S(1)}, f32[256]{0:T(256)S(1)}) all-reduce(f32[256]{0:T(256)S(1)} %copy-done.34, f32[256]{0:T(256)S(1)} %copy-done.30), channel_id=1, replica_groups=mesh['parts'=2,'row'=16] {'row'}, use_global_device_ids=true, to_apply=%region_13.15 | all-reduce | flops 512 | bytes 4096 | tf_op jit(solution)/shard_map/psum | solution.py:146
  260.2 3.9 %fusion.25 = bf16[1024,256]{0,1:T(8,128)(2,1)} fusion(f32[1024,256]{0,1:T(8,128)} %copy.52, bf16[1024,256]{0,1:T(8,128)(2,1)} %copy-done.3, bf16[1024,256]{0,1:T(8,128)(2,1)} %collective-permute-done.7, bf16[1024,256]{0,1:T(8,128)(2,1)} %collective-permute-done.6, f32[3072,256]{0,1:T(8,128)S(1)} %copy-done.2, bf16[1024,256]{0,1:T(8,128)(2,1)} %collective-permute-done.5, ...), kind=kLoop, calls=%fused_computation.45 | loop fusion | flops 3407872 | bytes 6291456 | tf_op jit(solution)/shard_map/convert_element_type | solution.py:142
  264.1 2.0 copy.44
  266.1 21.8 %all-reduce.4.cloned.1.call-done = (f32[768,256]{1,0:T(8,128)}, f32[256,256]{1,0:T(8,128)}, f32[512,256]{1,0:T(8,128)}, f32[256,256]{1,0:T(8,128)}) async-done(((f32[768,256]{1,0:T(8,128)}, f32[256,256]{1,0:T(8,128)}, f32[512,256]{1,0:T(8,128)}, f32[256,256]{1,0:T(8,128)}), (f32[768,256]{1,0:T(8,128)}, f32[256,256]{1,0:T(8,128)}, f32[512,256]{1,0:T(8,128)}, ...) | async-done | bytes 1835024 | tf_op jit(solution)/shard_map/psum | solution.py:146
  287.9 2.1 broadcast_multiply_fusion
  290.0 1.9 broadcast_multiply_fusion.1
  291.9 0.7 broadcast_multiply_fusion.2
  292.6 0.7 broadcast_multiply_fusion.3
  (220 shorter events, 37.8 us)
Async XLA Ops:
  7.2 85.7 %copy-start = (bf16[768,256]{1,0:T(8,128)(2,1)S(1)}, bf16[768,256]{1,0:T(8,128)(2,1)}, u32[]{:S(2)}) copy-start(bf16[768,256]{1,0:T(8,128)(2,1)} %param.30) | copy-start | bytes 1179652
  7.2 280.7 %all-reduce.4.cloned.1.call-start = ((), (), s32[]{:S(2)}) async-start(), calls=%async_computation | async-start | bytes 3670016 | tf_op jit(solution)/shard_map/psum | solution.py:146
  9.4 2.7 copy-start.18
  9.5 2.7 copy-start.24
  12.1 1.2 copy-start.12
  12.1 1.4 copy-start.28
  13.6 2.0 copy-start.3
  13.6 1.4 copy-start.41
  15.0 1.4 copy-start.21
  16.4 1.0 copy-start.7
  16.8 9.5 %copy-start.9 = (bf16[1024,256]{1,0:T(8,128)(2,1)S(1)}, bf16[1024,256]{1,0:T(8,128)(2,1)}, u32[]{:S(2)}) copy-start(bf16[1024,256]{1,0:T(8,128)(2,1)} %copy-done.8) | copy-start | bytes 1572868
  16.9 10.4 %copy-start.38 = (s32[6]{0:T(128)S(1)}, s32[6]{0:T(128)}, u32[]{:S(2)}) copy-start(s32[6]{0:T(128)} %param.28) | copy-start | bytes 76
  16.9 10.4 %copy-start.36 = (s32[6]{0:T(128)S(1)}, s32[6]{0:T(128)}, u32[]{:S(2)}) copy-start(s32[6]{0:T(128)} %param.27) | copy-start | bytes 76
  16.9 11.1 %copy-start.32 = (s32[6,128]{1,0:T(8,128)S(1)}, s32[6,128]{1,0:T(8,128)}, u32[]{:S(2)}) copy-start(s32[6,128]{1,0:T(8,128)} %param.26) | copy-start | bytes 9220
  17.0 11.1 %copy-start.31 = (s32[6,128]{1,0:T(8,128)S(1)}, s32[6,128]{1,0:T(8,128)}, u32[]{:S(2)}) copy-start(s32[6,128]{1,0:T(8,128)} %param.25) | copy-start | bytes 9220
  18.5 67.8 %collective-permute-start.2 = (bf16[2,1024,256]{2,1,0:T(8,128)(2,1)}, bf16[2,1024,256]{2,1,0:T(8,128)(2,1)}, u32[]{:S(2)}, u32[]{:S(2)}) collective-permute-start(bf16[2,1024,256]{2,1,0:T(8,128)(2,1)} %get-tuple-element.172), channel_id=1, source_target_pairs={{1,0},{2,1},{3,2},{4,3},{5,4},{6,5},{7,6},{8,7},{9,8},{10,9},{11,1... | collective-permute-start | bytes 3145736 | tf_op jit(solution)/shard_map/ppermute | solution.py:12
  23.9 62.4 %collective-permute-start.3 = (bf16[2,1024,256]{2,1,0:T(8,128)(2,1)}, bf16[2,1024,256]{2,1,0:T(8,128)(2,1)}, u32[]{:S(2)}, u32[]{:S(2)}) collective-permute-start(bf16[2,1024,256]{2,1,0:T(8,128)(2,1)} %get-tuple-element.172), channel_id=1, source_target_pairs={{2,0},{3,1},{4,2},{5,3},{6,4},{7,5},{8,6},{9,7},{10,8},{11,9},{12,... | collective-permute-start | bytes 3145736 | tf_op jit(solution)/shard_map/ppermute | solution.py:12
  24.5 51.3 %collective-permute-start = (bf16[1024,256]{1,0:T(8,128)(2,1)S(1)}, bf16[1024,256]{1,0:T(8,128)(2,1)}, u32[]{:S(2)}, u32[]{:S(2)}) collective-permute-start(bf16[1024,256]{1,0:T(8,128)(2,1)S(1)} %copy-done.7), channel_id=1, source_target_pairs={{2,0},{3,1},{4,2},{5,3},{6,4},{7,5},{8,6},{9,7},{10,8},{11,9},{12,... | collective-permute-start | bytes 1572872 | tf_op jit(solution)/shard_map/ppermute | solution.py:12
  25.8 55.6 %collective-permute-start.1 = (bf16[1024,256]{1,0:T(8,128)(2,1)S(1)}, bf16[1024,256]{1,0:T(8,128)(2,1)}, u32[]{:S(2)}, u32[]{:S(2)}) collective-permute-start(bf16[1024,256]{1,0:T(8,128)(2,1)S(1)} %copy-done.7), channel_id=1, source_target_pairs={{4,0},{5,1},{6,2},{7,3},{8,4},{9,5},{10,6},{11,7},{12,8},{13,9},{1... | collective-permute-start | bytes 1572872 | tf_op jit(solution)/shard_map/ppermute | solution.py:12
  28.1 63.6 %copy-start.25 = (pred[768]{0:T(1024)(128)(4,1)}, pred[768]{0:T(1024)(128)(4,1)S(1)}, u32[]{:S(2)}) copy-start(pred[768]{0:T(1024)(128)(4,1)S(1)} %get-tuple-element.159) | copy-start | bytes 2308
  28.8 4.0 %copy-start.14 = (bf16[1024,256]{1,0:T(8,128)(2,1)S(1)}, bf16[1024,256]{1,0:T(8,128)(2,1)}, u32[]{:S(2)}) copy-start(bf16[1024,256]{1,0:T(8,128)(2,1)} %copy-done.13) | copy-start | bytes 1572868
  32.8 49.9 %copy-start.27 = (s32[1024]{0:T(1024)S(1)}, s32[1024]{0:T(1024)}, u32[]{:S(2)}) copy-start(s32[1024]{0:T(1024)} %pad_clamp_fusion.1) | copy-start | bytes 12292
  82.7 2.7 copy-start.29
  92.9 2.7 copy-start.16
  92.9 2.7 copy-start.22
  96.0 4.5 %copy-start.4 = (bf16[768,256]{0,1:T(8,128)(2,1)S(1)}, bf16[768,256]{0,1:T(8,128)(2,1)}, u32[]{:S(2)}) copy-start(bf16[768,256]{0,1:T(8,128)(2,1)} %copy.37) | copy-start | bytes 1179652
  99.3 3.1 %copy-start.26 = (pred[768]{0:T(1024)(128)(4,1)S(1)}, pred[768]{0:T(1024)(128)(4,1)}, u32[]{:S(2)}) copy-start(pred[768]{0:T(1024)(128)(4,1)} %copy-done.25) | copy-start | bytes 2308
  99.3 3.1 %copy-start.33 = (f32[256]{0:T(256)S(1)}, f32[256]{0:T(256)}, u32[]{:S(2)}) copy-start(f32[256]{0:T(256)} %param.32) | copy-start | bytes 3076
  100.5 3.7 %copy-start.6 = (bf16[768,256]{0,1:T(8,128)(2,1)}, bf16[768,256]{0,1:T(8,128)(2,1)S(1)}, u32[]{:S(2)}) copy-start(bf16[768,256]{0,1:T(8,128)(2,1)S(1)} %copy.38) | copy-start | bytes 1179652
  100.5 3.2 %copy-start.23 = (bf16[256,256]{1,0:T(8,128)(2,1)S(1)}, bf16[256,256]{1,0:T(8,128)(2,1)}, u32[]{:S(2)}) copy-start(bf16[256,256]{1,0:T(8,128)(2,1)} %param.31) | copy-start | bytes 393220
  100.5 3.2 %copy-start.42 = (f32[768,256]{1,0:T(8,128)S(1)}, f32[768,256]{1,0:T(8,128)}, u32[]{:S(2)}) copy-start(f32[768,256]{1,0:T(8,128)} %get-tuple-element.178) | copy-start | bytes 2359300
  103.7 1.1 copy-start.17
  103.7 1.2 copy-start.35
  110.2 2.1 copy-start.37
  110.2 2.1 copy-start.39
  112.3 4.0 %copy-start.10 = (bf16[6,128,256]{2,1,0:T(8,128)(2,1)}, bf16[6,128,256]{2,1,0:T(8,128)(2,1)S(1)}, u32[]{:S(2)}) copy-start(bf16[6,128,256]{2,1,0:T(8,128)(2,1)S(1)} %get-tuple-element.275) | copy-start | bytes 1179652 | tf_op jit(solution)/shard_map/while
  121.0 1.6 copy-start.11
  121.0 1.6 copy-start.40
  122.6 4.0 %copy-start.10 = (bf16[6,128,256]{2,1,0:T(8,128)(2,1)}, bf16[6,128,256]{2,1,0:T(8,128)(2,1)S(1)}, u32[]{:S(2)}) copy-start(bf16[6,128,256]{2,1,0:T(8,128)(2,1)S(1)} %get-tuple-element.275) | copy-start | bytes 1179652 | tf_op jit(solution)/shard_map/while
  131.3 1.6 copy-start.11
  131.3 1.6 copy-start.40
  132.9 4.0 %copy-start.10 = (bf16[6,128,256]{2,1,0:T(8,128)(2,1)}, bf16[6,128,256]{2,1,0:T(8,128)(2,1)S(1)}, u32[]{:S(2)}) copy-start(bf16[6,128,256]{2,1,0:T(8,128)(2,1)S(1)} %get-tuple-element.275) | copy-start | bytes 1179652 | tf_op jit(solution)/shard_map/while
  141.6 1.5 copy-start.11
  141.6 1.5 copy-start.40
  143.1 4.0 %copy-start.10 = (bf16[6,128,256]{2,1,0:T(8,128)(2,1)}, bf16[6,128,256]{2,1,0:T(8,128)(2,1)S(1)}, u32[]{:S(2)}) copy-start(bf16[6,128,256]{2,1,0:T(8,128)(2,1)S(1)} %get-tuple-element.275) | copy-start | bytes 1179652 | tf_op jit(solution)/shard_map/while
  151.8 1.6 copy-start.11
  151.9 1.6 copy-start.40
  153.4 4.0 %copy-start.10 = (bf16[6,128,256]{2,1,0:T(8,128)(2,1)}, bf16[6,128,256]{2,1,0:T(8,128)(2,1)S(1)}, u32[]{:S(2)}) copy-start(bf16[6,128,256]{2,1,0:T(8,128)(2,1)S(1)} %get-tuple-element.275) | copy-start | bytes 1179652 | tf_op jit(solution)/shard_map/while
  162.1 1.6 copy-start.11
  162.1 1.6 copy-start.40
  163.7 4.0 %copy-start.10 = (bf16[6,128,256]{2,1,0:T(8,128)(2,1)}, bf16[6,128,256]{2,1,0:T(8,128)(2,1)S(1)}, u32[]{:S(2)}) copy-start(bf16[6,128,256]{2,1,0:T(8,128)(2,1)S(1)} %get-tuple-element.275) | copy-start | bytes 1179652 | tf_op jit(solution)/shard_map/while
  172.4 1.6 copy-start.11
  172.4 1.6 copy-start.40
  174.0 3.3 %copy-start.2 = (f32[3072,256]{0,1:T(8,128)S(1)}, f32[3072,256]{0,1:T(8,128)}, u32[]{:S(2)}) copy-start(f32[3072,256]{0,1:T(8,128)} %get-tuple-element.304) | copy-start | bytes 9437188
  177.3 82.8 %collective-permute-start.4 = (bf16[1024,256]{0,1:T(8,128)(2,1)}, bf16[1024,256]{0,1:T(8,128)(2,1)}, u32[]{:S(2)}, u32[]{:S(2)}) collective-permute-start(bf16[1024,256]{0,1:T(8,128)(2,1)} %get-tuple-element.165), channel_id=1, source_target_pairs={{15,0},{0,1},{1,2},{2,3},{3,4},{4,5},{5,6},{6,7},{7,8},{8,9},{9,10... | collective-permute-start | bytes 1572872 | tf_op jit(solution)/shard_map/ppermute | solution.py:12
  177.3 82.8 %collective-permute-start.5 = (bf16[1024,256]{0,1:T(8,128)(2,1)}, bf16[1024,256]{0,1:T(8,128)(2,1)}, u32[]{:S(2)}, u32[]{:S(2)}) collective-permute-start(bf16[1024,256]{0,1:T(8,128)(2,1)} %get-tuple-element.166), channel_id=1, source_target_pairs={{14,0},{15,1},{0,2},{1,3},{2,4},{3,5},{4,6},{5,7},{6,8},{7,9},{8,1... | collective-permute-start | bytes 1572872 | tf_op jit(solution)/shard_map/ppermute | solution.py:12
  177.6 4.6 %copy-start.5 = (bf16[768,256]{0,1:T(8,128)(2,1)S(1)}, bf16[768,256]{0,1:T(8,128)(2,1)}, u32[]{:S(2)}) copy-start(bf16[768,256]{0,1:T(8,128)(2,1)} %copy.37) | copy-start | bytes 1179652
  178.6 7.7 %copy-start.30 = (f32[256]{0:T(256)S(1)}, f32[256]{0:T(256)}, u32[]{:S(2)}) copy-start(f32[256]{0:T(256)} %get-tuple-element.129) | copy-start | bytes 3076
  178.6 7.7 %copy-start.34 = (f32[256]{0:T(256)S(1)}, f32[256]{0:T(256)}, u32[]{:S(2)}) copy-start(f32[256]{0:T(256)} %get-tuple-element.127) | copy-start | bytes 3076
  178.6 81.5 %collective-permute-start.6 = (bf16[1024,256]{0,1:T(8,128)(2,1)}, bf16[1024,256]{0,1:T(8,128)(2,1)}, u32[]{:S(2)}, u32[]{:S(2)}) collective-permute-start(bf16[1024,256]{0,1:T(8,128)(2,1)} %get-tuple-element.167), channel_id=1, source_target_pairs={{14,0},{15,1},{0,2},{1,3},{2,4},{3,5},{4,6},{5,7},{6,8},{7,9},{8,1... | collective-permute-start | bytes 1572872 | tf_op jit(solution)/shard_map/ppermute | solution.py:12
  180.6 79.5 %collective-permute-start.7 = (bf16[1024,256]{0,1:T(8,128)(2,1)}, bf16[1024,256]{0,1:T(8,128)(2,1)}, u32[]{:S(2)}, u32[]{:S(2)}) collective-permute-start(bf16[1024,256]{0,1:T(8,128)(2,1)} %get-tuple-element.168), channel_id=1, source_target_pairs={{12,0},{13,1},{14,2},{15,3},{0,4},{1,5},{2,6},{3,7},{4,8},{5,9},{6... | collective-permute-start | bytes 1572872 | tf_op jit(solution)/shard_map/ppermute | solution.py:12
  260.2 33.2 %copy-start.1 = (bf16[768,256]{1,0:T(8,128)(2,1)S(1)}, bf16[768,256]{1,0:T(8,128)(2,1)}, u32[]{:S(2)}) copy-start(bf16[768,256]{1,0:T(8,128)(2,1)} %param.30) | copy-start | bytes 1179652
  287.9 4.0 %copy-start.20 = (f32[256,256]{1,0:T(8,128)S(1)}, f32[256,256]{1,0:T(8,128)}, u32[]{:S(2)}) copy-start(f32[256,256]{1,0:T(8,128)} %get-tuple-element.156) | copy-start | bytes 786436
  287.9 4.7 %copy-start.19 = (f32[256,256]{1,0:T(8,128)S(1)}, f32[256,256]{1,0:T(8,128)}, u32[]{:S(2)}) copy-start(f32[256,256]{1,0:T(8,128)} %get-tuple-element.154) | copy-start | bytes 786436
  (3 other events, 2.6 us)
Sparse Core Ops, SparseCore 0:
  182.3 105.5 all-reduce.3
where the time goes:
time: 302 us; the launch traced here: 300 us
  local copies, waits for them, and re-layouts  80.3 us (27%)
  blocking collectives  72.7 us (24%)
  waiting for transfers between devices  67.8 us (22%)
  other arithmetic  26.5 us (9%)
  matrix products  17.7 us (6%)
  between operations  15.2 us (5%)
  starting transfers between devices  11.4 us (4%)
  loops' own time  8.74 us (3%)
    psum x1, blocking collectives, on_device(): lax.psum((edge_gw_in, edge_gw_out, edge_g_gain, node_gw_in, node_gw_out,...  72.7 us
    ppermute x8, waiting for transfers between devices, passed_along(): return lax.ppermute(block, axis, route)  46 us
    psum x1, waiting for transfers between devices, on_device(): lax.psum((edge_gw_in, edge_gw_out, edge_g_gain, node_gw_in, node_gw_out,...  21.8 us
    dynamic_slice x24, local copies, waits for them, and re-layouts, add_block(): current = lax.dynamic_slice_in_dim(accum, start_row, block_rows, 0)  19.6 us
    dynamic_update_slice x18, local copies, waits for them, and re-layouts, add_block(): lax.dynamic_update_slice_in_dim(accum, current + tile_term, start_row, 0)  13.2 us
    unnamed x87, local copies, waits for them, and re-layouts  12.7 us
    ppermute x8, starting transfers between devices, passed_along(): return lax.ppermute(block, axis, route)  11.3 us
    another operation x1, loops' own time, on_device(): lax.scan(add_tile, (empty_sums, empty_sums), (send_slot, send_local, send...  8.74 us
  transfers between devices with their start and end apart: 9, of which 3 were waited for; matrix products, arithmetic and copies ran while one was open for 9% of the time, Pallas kernels for 0%

commit v1 on v0

v1 whole, which is shorter than its diff:
```python
import functools
import jax
import jax.numpy as jnp
from jax import lax
from jax.experimental import pallas as pl
from jax.experimental.pallas import tpu as pltpu
from jax.sharding import PartitionSpec as P

EPSILON = 1e-05
F32 = jnp.float32
BF16 = jnp.bfloat16
INNER = 4


def mm(a, b):
    return jnp.dot(a, b, preferred_element_type=F32)


def mm_nt(a, b):
    return lax.dot_general(a, b, (((1,), (1,)), ((), ())), preferred_element_type=F32)


def mm_tn(a, b):
    return lax.dot_general(a, b, (((0,), (0,)), ((), ())), preferred_element_type=F32)


def norm_backward(output, cotangent, gain):
    row_mean = jnp.mean(output, axis=-1, keepdims=True)
    centred = output - row_mean
    inverse = lax.rsqrt(jnp.mean(centred * centred, axis=-1, keepdims=True) + EPSILON)
    normed = centred * inverse
    grad_gain = jnp.sum(cotangent * normed, axis=0, keepdims=True)
    scaled = cotangent * gain
    out_grad = inverse * (
        scaled
        - jnp.mean(scaled, axis=-1, keepdims=True)
        - normed * jnp.mean(scaled * normed, axis=-1, keepdims=True)
    )
    return out_grad.astype(BF16), grad_gain


def pick(slot, options):
    return lax.select(slot == 0, options[0], lax.select(slot == 1, options[1], options[2]))


def layer_kernel(
    n,
    stride,
    fused,
    node_scale,
    edge_scale,
    x_ref,
    agg_ref,
    ncot_ref,
    e_ref,
    ecot_ref,
    sloc_ref,
    rloc_ref,
    sslot_ref,
    rslot_ref,
    count_ref,
    ewi_ref,
    ewo_ref,
    eg_ref,
    nwi_ref,
    nwo_ref,
    ng_ref,
    ngrad_ref,
    egrad_ref,
    egw_ref,
    ngw_ref,
    gains_ref,
    req,
    req_in,
    onehot,
    lat_out,
    lat_in,
    agg_out,
    agg_in,
    ret_out,
    ret_in,
    n_act,
    n_dout,
    n_dpre,
    n_agg,
    n_base,
    snd,
    rcv,
    e_pre,
    e_act,
    e_out,
    e_dout,
    e_dpre,
    gain_acc,
    w_src,
    w_a,
    w_sum,
    w_b_src,
    w_b,
    w_fin,
    g_a,
    g_b,
    send_sem,
    recv_sem,
):
    nb, h = x_ref.shape
    edges = e_ref.shape[0]
    tile = sloc_ref.shape[1]
    me = lax.axis_index("row")
    group = 4 * tile
    steps = [s for s in (1, 2)]
    hops = [0, stride, 2 * stride, 0, 1, 2]
    remote = (1, 2, 4, 5)
    outer = n // INNER
    ia, ib = lax.rem(me, INNER), me // INNER

    def at(offset):
        return lax.rem(me + offset % n, n)

    def inner_peer(i):
        return ib * INNER + lax.rem(ia + i, INNER)

    def outer_peer(i):
        return lax.rem(ib + i, outer) * INNER + ia

    partners = [at(o) for o in sorted({k for s in (1, 2) for d in (1, stride) for k in (s * d % n, -s * d % n)})]
    if fused:
        partners += [inner_peer(i) for i in range(1, INNER)]
        partners += [outer_peer(i) for i in range(1, outer)]
    barrier = pltpu.get_barrier_semaphore()
    for p in partners:
        pl.semaphore_signal(barrier, inc=1, device_id={"row": p}, device_id_type=pl.DeviceIdType.MESH)

    used = [0]

    def remote_copy(src, dst, target):
        k = used[0]
        used[0] += 1
        copy = pltpu.make_async_remote_copy(
            src_ref=src,
            dst_ref=dst,
            send_sem=send_sem.at[k],
            recv_sem=recv_sem.at[k],
            device_id={"row": target},
            device_id_type=pl.DeviceIdType.MESH,
        )
        copy.start()
        return copy

    for side, (loc, slot) in enumerate(((sloc_ref, sslot_ref), (rloc_ref, rslot_ref))):
        tiles = [loc[j : j + 1, :] for j in range(6)]
        none = jnp.full((1, tile), -1, jnp.int32)
        for s in range(3):
            k = side * 3 + s
            lead = lax.select(slot[0] == s, tiles[0], lax.select(slot[1] == s, tiles[1], tiles[2]))
            req[k, :, 0:tile] = lead
            for j in range(3):
                req[k, :, tile * (j + 1) : tile * (j + 2)] = lax.select(slot[3 + j] == s, tiles[3 + j], none)

    pl.semaphore_wait(barrier, len(partners))
    asks = {k: remote_copy(req.at[k], req_in.at[k], at(hops[k])) for k in remote}

    def make_onehot(k, index_ref):
        index = index_ref[k]

        def rows(i, carry):
            r = pl.multiple_of(i * 128, 128)
            ids = lax.broadcasted_iota(jnp.int32, (128, group), 0) + r
            onehot[k, pl.ds(r, 128), :] = (ids == index).astype(F32).astype(BF16)
            return carry

        lax.fori_loop(0, nb // 128, rows, 0)

    for k in (0, 3):
        make_onehot(k, req)
        lat_in[k] = mm_tn(onehot[k], x_ref[...]).astype(BF16)
    lats = {}
    for k in (2, 5, 1, 4):
        asks[k].wait()
        make_onehot(k, req_in)
        lat_out[k] = mm_tn(onehot[k], x_ref[...]).astype(BF16)
        lats[k] = remote_copy(lat_out.at[k], lat_in.at[k], at(-hops[k]))

    gain_acc[...] = jnp.zeros_like(gain_acc)

    def node_rows(i, carry):
        r = pl.ds(pl.multiple_of(i * 256, 256), 256)
        pre = mm(x_ref[r, :], nwi_ref[0:h, :]) + mm(agg_ref[r, :], nwi_ref[h:, :])
        sig = lax.logistic(pre)
        act = (pre * sig).astype(BF16)
        n_act[r, :] = act
        cot = ncot_ref[r, :].astype(F32)
        dout, gg = norm_backward(mm(act, nwo_ref[...]), cot, ng_ref[...])
        gain_acc[8:9, :] += gg
        n_dout[r, :] = dout
        dpre = (mm_nt(dout, nwo_ref[...]) * sig * (1.0 + pre * (1.0 - sig))).astype(BF16)
        n_dpre[r, :] = dpre
        n_agg[r, :] = mm_nt(dpre, nwi_ref[h:, :]).astype(BF16)
        n_base[r, :] = cot + mm_nt(dpre, nwi_ref[0:h, :])
        return carry

    lax.fori_loop(0, nb // 256, node_rows, 0)
    aggs = {}
    for s in (2, 1):
        agg_out[s] = mm_tn(onehot[3 + s], n_agg[...]).astype(BF16)
        aggs[s] = remote_copy(agg_out.at[s], agg_in.at[s], at(-s))
    agg_in[0] = mm_tn(onehot[3], n_agg[...]).astype(BF16)

    def rows_of(lo, rows, part):
        return pl.ds(pl.multiple_of(lo + part * rows, 16), rows)

    class Sum:
        def __init__(self, lo, total, scale, full):
            self.lo, self.total, self.scale, self.full = lo, total, scale, full
            self.q = total // INNER
            self.e = self.q // outer
            self.qlo, self.elo = lo // INNER, lo // INNER // outer

        def start_a(self):
            w_src[self.lo : self.lo + self.total, :] = self.full[...].astype(BF16)
            self.copies = [
                remote_copy(
                    w_src.at[rows_of(self.lo, self.q, lax.rem(ia + i, INNER)), :],
                    w_a.at[i - 1, pl.ds(self.qlo, self.q), :],
                    inner_peer(i),
                )
                for i in range(1, INNER)
            ]

        def start_b(self):
            for c in self.copies:
                c.wait()
            total = self.full[rows_of(0, self.q, ia), :]
            mine = pl.ds(self.qlo, self.q)
            for i in range(INNER - 1):
                total = total + w_a[i, mine, :].astype(F32)
            w_sum[mine, :] = total
            w_b_src[mine, :] = total.astype(BF16)
            self.copies = [
                remote_copy(
                    w_b_src.at[rows_of(self.qlo, self.e, lax.rem(ib + i, outer)), :],
                    w_b.at[i - 1, pl.ds(self.elo, self.e), :],
                    outer_peer(i),
                )
                for i in range(1, outer)
            ]

        def start_c(self):
            for c in self.copies:
                c.wait()
            total = w_sum[rows_of(self.qlo, self.e, ib), :]
            for i in range(outer - 1):
                total = total + w_b[i, pl.ds(self.elo, self.e), :].astype(F32)
            piece = pl.ds(pl.multiple_of(self.lo + ia * self.q + ib * self.e, 16), self.e)
            w_fin[piece, :] = (total * self.scale).astype(BF16)
            self.copies = [
                remote_copy(w_fin.at[piece, :], w_fin.at[piece, :], outer_peer(i)) for i in range(1, outer)
            ]

        def start_d(self):
            for c in self.copies:
                c.wait()
            piece = rows_of(self.lo, self.q, ia)
            self.copies = [
                remote_copy(w_fin.at[piece, :], w_fin.at[piece, :], inner_peer(i)) for i in range(1, INNER)
            ]

        def finish(self):
            for c in self.copies:
                c.wait()
            self.full[...] = w_fin[self.lo : self.lo + self.total, :].astype(F32)

    n_total = ngw_ref.shape[0]
    e_total = egw_ref.shape[0]
    edge_sum = Sum(0, e_total, edge_scale, egw_ref)
    node_sum = Sum(e_total, n_total, node_scale, ngw_ref)
    ngw_ref[0:h, :] = mm_tn(x_ref[...], n_dpre[...])
    ngw_ref[h : 2 * h, :] = mm_tn(agg_ref[...], n_dpre[...])
    ngw_ref[2 * h :, :] = mm_tn(n_act[...], n_dout[...])
    if fused:
        node_sum.start_a()

    def unpack(side, slot, buffer, table):
        for j in range(6):
            lo = 0 if j < 3 else tile * (j - 2)
            options = [buffer[side * 3 + s, lo : lo + tile, :] for s in range(3)]
            table[j * tile : (j + 1) * tile, :] = pick(slot[j], options)

    for k in (2, 1):
        lats[k].wait()
    unpack(0, sslot_ref, lat_in, snd)
    for k in (5, 4):
        lats[k].wait()
    unpack(1, rslot_ref, lat_in, rcv)
    if fused:
        node_sum.start_b()

    def edge_forward(i, carry):
        r = pl.ds(pl.multiple_of(i * 256, 256), 256)
        pre = mm(e_ref[r, :], ewi_ref[0:h, :]) + mm(snd[r, :], ewi_ref[h : 2 * h, :]) + mm(rcv[r, :], ewi_ref[2 * h :, :])
        e_pre[r, :] = pre
        act = (pre * lax.logistic(pre)).astype(BF16)
        e_act[r, :] = act
        e_out[r, :] = mm(act, ewo_ref[...])
        return carry

    lax.fori_loop(0, edges // 256, edge_forward, 0)
    if fused:
        node_sum.start_c()
    for s in (2, 1):
        aggs[s].wait()
    unpack(0, rslot_ref, agg_in, e_dpre)
    live_rows = count_ref[0] * tile

    def edge_backward(i, carry):
        lo = pl.multiple_of(i * 256, 256)
        r = pl.ds(lo, 256)
        live = (lax.broadcasted_iota(jnp.int32, (256, h), 0) + lo) < live_rows
        cot = jnp.where(live, ecot_ref[r, :].astype(F32) + e_dpre[r, :].astype(F32), 0.0)
        dout, gg = norm_backward(e_out[r, :], cot, eg_ref[...])
        gain_acc[0:1, :] += gg
        e_dout[r, :] = dout
        pre = e_pre[r, :]
        sig = lax.logistic(pre)
        dpre = (mm_nt(dout, ewo_ref[...]) * sig * (1.0 + pre * (1.0 - sig))).astype(BF16)
        e_dpre[r, :] = dpre
        egrad_ref[r, :] = (cot + mm_nt(dpre, ewi_ref[0:h, :])).astype(BF16)
        e_out[r, :] = mm_nt(dpre, ewi_ref[h : 2 * h, :])
        e_pre[r, :] = mm_nt(dpre, ewi_ref[2 * h :, :])
        return carry

    lax.fori_loop(0, edges // 256, edge_backward, 0)

    rets = {}
    for k in (2, 5, 1, 4, 0, 3):
        s = k % 3
        grads, slot = (e_out, sslot_ref) if k < 3 else (e_pre, rslot_ref)
        target = ret_in if s == 0 else ret_out
        lead = [grads[j * tile : (j + 1) * tile, :] for j in range(3)]
        lead = lax.select(slot[0] == s, lead[0], lax.select(slot[1] == s, lead[1], lead[2]))
        target[k, 0:tile, :] = lead.astype(BF16)
        target[k, tile:, :] = grads[3 * tile :, :].astype(BF16)
        if s:
            rets[k] = remote_copy(ret_out.at[k], ret_in.at[k], at(hops[k]))

    if fused:
        node_sum.start_d()
    egw_ref[0:h, :] = mm_tn(e_ref[...], e_dpre[...])
    egw_ref[h : 2 * h, :] = mm_tn(snd[...], e_dpre[...])
    egw_ref[2 * h : 3 * h, :] = mm_tn(rcv[...], e_dpre[...])
    egw_ref[3 * h :, :] = mm_tn(e_act[...], e_dout[...])
    if fused:
        edge_sum.start_a()
        g_a[ia] = gain_acc[...]
        gains = [remote_copy(gain_acc, g_a.at[ia], inner_peer(i)) for i in range(1, INNER)]

    n_base[...] += mm(onehot[0], ret_in[0]) + mm(onehot[3], ret_in[3])
    if fused:
        node_sum.finish()
        edge_sum.start_b()
        for c in gains:
            c.wait()
        g_sum = g_a[0]
        for i in range(1, INNER):
            g_sum = g_sum + g_a[i]
        gain_acc[...] = g_sum
        g_b[ib] = g_sum
        gains = [remote_copy(gain_acc, g_b.at[ib], outer_peer(i)) for i in range(1, outer)]
        edge_sum.start_c()
    for k in (1, 4):
        rets[k].wait()
    n_base[...] += mm(onehot[1], ret_in[1]) + mm(onehot[4], ret_in[4])
    if fused:
        edge_sum.start_d()
    for k in (2, 5):
        rets[k].wait()
    total = n_base[...] + mm(onehot[2], ret_in[2]) + mm(onehot[5], ret_in[5])
    ngrad_ref[...] = total.astype(BF16)
    if fused:
        for c in gains:
            c.wait()
        g_sum = g_b[0]
        for i in range(1, outer):
            g_sum = g_sum + g_b[i]
        gains_ref[0:8, :] = g_sum[0:8, :] * edge_scale
        gains_ref[8:16, :] = g_sum[8:16, :] * node_scale
        edge_sum.finish()
    else:
        gains_ref[...] = gain_acc[...]


def on_device(
    node_latent,
    agg_saved,
    node_cot,
    edge_latent,
    edge_cot,
    send_local,
    recv_local,
    send_slot,
    recv_slot,
    tile_count,
    edge_w_in,
    edge_w_out,
    edge_gain,
    node_w_in,
    node_w_out,
    node_gain,
):
    nb, h = node_latent.shape
    edges = edge_latent.shape[0]
    tile_total, tile = send_local.shape
    n = lax.axis_size("row")
    stride = n // 8
    node_scale = (nb * n) ** (-0.5)
    edge_scale = (edges * n) ** (-0.5)
    outer = n // INNER
    fused = n % INNER == 0 and 3 * h % (INNER * outer * 16) == 0 and 4 * h % (INNER * outer * 16) == 0
    levels = outer if fused else 2
    group = 4 * tile
    weights = 7 * h
    vmem = pl.BlockSpec(memory_space=pltpu.VMEM)
    smem = pl.BlockSpec(memory_space=pltpu.SMEM)
    copies = 14 + (2 * (2 * (INNER - 1) + 2 * (outer - 1)) + INNER - 1 + outer - 1 if fused else 0)
    node_grad, edge_grad, egw, ngw, gains = pl.pallas_call(
        functools.partial(layer_kernel, n, stride, fused, node_scale, edge_scale),
        out_shape=(
            jax.ShapeDtypeStruct((nb, h), BF16),
            jax.ShapeDtypeStruct((edges, h), BF16),
            jax.ShapeDtypeStruct((4 * h, h), F32),
            jax.ShapeDtypeStruct((3 * h, h), F32),
            jax.ShapeDtypeStruct((16, h), F32),
        ),
        in_specs=[vmem] * 7 + [smem] * 3 + [vmem] * 6,
        out_specs=(vmem,) * 5,
        scratch_shapes=[
            pltpu.VMEM((6, 1, group), jnp.int32),
            pltpu.VMEM((6, 1, group), jnp.int32),
            pltpu.VMEM((6, nb, group), BF16),
            pltpu.VMEM((6, group, h), BF16),
            pltpu.VMEM((6, group, h), BF16),
            pltpu.VMEM((3, group, h), BF16),
            pltpu.VMEM((3, group, h), BF16),
            pltpu.VMEM((6, group, h), BF16),
            pltpu.VMEM((6, group, h), BF16),
            pltpu.VMEM((nb, h), BF16),
            pltpu.VMEM((nb, h), BF16),
            pltpu.VMEM((nb, h), BF16),
            pltpu.VMEM((nb, h), BF16),
            pltpu.VMEM((nb, h), F32),
            pltpu.VMEM((edges, h), BF16),
            pltpu.VMEM((edges, h), BF16),
            pltpu.VMEM((edges, h), F32),
            pltpu.VMEM((edges, h), BF16),
            pltpu.VMEM((edges, h), F32),
            pltpu.VMEM((edges, h), BF16),
            pltpu.VMEM((edges, h), BF16),
            pltpu.VMEM((16, h), F32),
            pltpu.VMEM((weights, h), BF16),
            pltpu.VMEM((INNER - 1, weights // INNER, h), BF16),
            pltpu.VMEM((weights // INNER, h), F32),
            pltpu.VMEM((weights // INNER, h), BF16),
            pltpu.VMEM((levels - 1, weights // INNER // levels, h), BF16),
            pltpu.VMEM((weights, h), BF16),
            pltpu.VMEM((INNER, 16, h), F32),
            pltpu.VMEM((levels, 16, h), F32),
            pltpu.SemaphoreType.DMA((copies,)),
            pltpu.SemaphoreType.DMA((copies,)),
        ],
        compiler_params=pltpu.CompilerParams(
            collective_id=0, has_side_effects=True, vmem_limit_bytes=50 * 1024 * 1024
        ),
        cost_estimate=pl.CostEstimate(flops=7 * 10**9, bytes_accessed=8 * 10**6, transcendentals=10**6),
    )(
        node_latent,
        agg_saved,
        node_cot,
        edge_latent,
        edge_cot,
        send_local,
        recv_local,
        send_slot,
        recv_slot,
        tile_count,
        edge_w_in,
        edge_w_out,
        edge_gain[None, :],
        node_w_in,
        node_w_out,
        node_gain[None, :],
    )
    if not fused:
        egw, ngw, gains = lax.psum((egw * edge_scale, ngw * node_scale, gains), "row")
        gains = gains * jnp.repeat(jnp.array([edge_scale, node_scale], F32), 8)[:, None]
    return (
        node_grad,
        edge_grad,
        egw[: 3 * h],
        egw[3 * h :],
        gains[0],
        ngw[: 2 * h],
        ngw[2 * h :],
        gains[8],
    )


def solution(mesh):
    placed = (P(("parts", "row"), None),) * 7 + (P(("parts", "row")),) * 3 + (P(),) * 6
    return jax.shard_map(
        on_device,
        mesh=mesh,
        in_specs=placed,
        out_specs=(
            P(("parts", "row"), None),
            P(("parts", "row"), None),
            P("parts", None),
            P("parts", None),
            P("parts"),
            P("parts", None),
            P("parts", None),
            P("parts"),
        ),
        check_vma=False,
    )
```

time: 302 us -> 112 us (0.37)
  Pallas kernels: 0 us -> 91.4 us
  blocking collectives: 72.7 us -> 0 us
  waiting for transfers between devices: 67.8 us -> 0 us
  local copies, waits for them, and re-layouts: 80.3 us -> 18 us
  other arithmetic: 26.5 us -> 0 us
  matrix products: 17.7 us -> 0 us
  between operations: 15.2 us -> 1.35 us
  starting transfers between devices: 11.4 us -> 0 us
  loops' own time: 8.74 us -> 0 us
    pallas_call x0 -> x1, Pallas kernels: none -> 91.4 us  [on_device(): pl.pallas_call(functools.partial(layer_kernel, n, stride, fused, node_sca...]
    psum x1 -> x0, blocking collectives: 72.7 us -> none  [on_device(): lax.psum((edge_gw_in, edge_gw_out, edge_g_gain, node_gw_in, node_gw_out,...]
    ppermute x8 -> x0, waiting for transfers between devices: 46 us -> none  [passed_along(): return lax.ppermute(block, axis, route)]
    dynamic_slice x36 -> x0, local copies, waits for them, and re-layouts: 27.7 us -> none  [the longest x24 19.6 us: add_block(): current = lax.dynamic_slice_in_dim(accum, start_row, block_rows, 0)]
    psum x1 -> x0, waiting for transfers between devices: 21.8 us -> none  [on_device(): lax.psum((edge_gw_in, edge_gw_out, edge_g_gain, node_gw_in, node_gw_out,...]
    dot_general x24 -> x0, matrix products: 17.7 us -> none  [the longest x2 5.3 us: mlp_backward(): preact = jnp.dot(inputs, w_in, preferred_element_type=jnp.float32)]
    dynamic_update_slice x18 -> x0, local copies, waits for them, and re-layouts: 13.2 us -> none  [add_block(): lax.dynamic_update_slice_in_dim(accum, current + tile_term, start_row, 0)]
    ppermute x8 -> x0, starting transfers between devices: 11.3 us -> none  [passed_along(): return lax.ppermute(block, axis, route)]
  transfers between devices with their start and end apart: 9 -> 0, of which waited for: 3 -> 0; matrix products, arithmetic and copies ran while one was open for 9% -> 0% of each run, Pallas kernels for 0% -> 0%
where the time goes in v1:
time: 112 us; the launch traced here: 111 us
  Pallas kernels  91.4 us (82%)
  local copies, waits for them, and re-layouts  18 us (16%)
  between operations  1.35 us (1%)
    pallas_call x1, Pallas kernels, on_device(): pl.pallas_call(functools.partial(layer_kernel, n, stride, fused, node_sca...  91.4 us
    unnamed x32, local copies, waits for them, and re-layouts  12 us

profile of v1, /device:TPU:0, one launch (start us, length us, event | category | flops | bytes accessed | tf_op | source)
XLA Modules:
  0.0 110.7 jit_solution(15296023236249721913)
XLA Ops:
  0.6 0.0 copy-start.8
  1.3 0.0 copy-start.10
  1.3 0.0 copy-start.12
  1.3 0.0 copy-done.8
  1.3 0.7 copy-done.10
  2.0 0.0 copy-done.12
  2.0 0.0 copy-start
  2.0 1.0 copy-done
  3.0 0.0 copy-start.1
  3.0 1.0 copy-done.1
  4.1 0.0 copy-start.2
  4.1 1.0 copy-done.2
  5.1 0.0 copy-start.3
  5.1 1.0 copy-done.3
  6.1 0.0 copy-start.4
  6.1 1.0 copy-done.4
  7.1 0.0 copy-start.5
  7.1 0.9 copy-done.5
  8.0 0.0 copy-start.6
  8.0 0.9 copy-done.6
  8.9 0.0 copy-start.7
  8.9 0.9 copy-done.7
  9.8 0.0 copy-start.9
  9.8 0.7 copy-done.9
  10.5 0.0 copy-start.11
  10.5 0.7 copy-done.11
  11.2 0.0 copy-start.13
  11.2 0.7 copy-done.13
  11.8 91.4 %shard_map.215 = (bf16[1024,256]{1,0:T(8,128)(2,1)S(1)}, bf16[768,256]{1,0:T(8,128)(2,1)S(1)}, f32[1024,256]{1,0:T(8,128)}, f32[768,256]{1,0:T(8,128)}, f32[16,256]{1,0:T(8,128)S(1)}) custom-call(bf16[1024,256]{1,0:T(8,128)(2,1)S(1)} %copy-done, bf16[1024,256]{1,0:T(8,128)(2,1)S(1)} %copy-done.1, bf16[1024,256]{1,0:T(8,128)(2,1)} %ncot_ref.1, ...), custom_call_target="tpu_custom_call" | custom-call | flops 7000000000 | bytes 8000000 | tf_op jit(solution)/shard_map/pallas_call | solution.py:425
  103.3 0.6 fusion
  103.9 1.7 %slice.19 = f32[256,256]{1,0:T(8,128)} slice(f32[1024,256]{1,0:T(8,128)} %get-tuple-element.15), slice={[768:1024], [0:256]} | slice | bytes 524288 | tf_op jit(solution)/shard_map/slice | solution.py:499
  105.5 0.0 copy-start.14
  105.5 2.1 %slice.18 = f32[768,256]{1,0:T(8,128)} slice(f32[1024,256]{1,0:T(8,128)} %get-tuple-element.15), slice={[0:768], [0:256]} | slice | bytes 1572864 | tf_op jit(solution)/shard_map/slice | solution.py:498
  107.7 0.0 copy-done.14
  107.7 0.7 slice.22
  108.4 0.8 slice.21
  109.2 0.8 copy.27
  110.0 0.7 copy.28
Async XLA Ops:
  0.6 0.7 copy-start.8
  1.3 0.7 copy-start.10
  1.3 0.7 copy-start.12
  2.0 1.0 copy-start
  3.0 1.0 copy-start.1
  4.1 1.0 copy-start.2
  5.1 1.0 copy-start.3
  6.1 1.0 copy-start.4
  7.1 0.9 copy-start.5
  8.0 0.9 copy-start.6
  8.9 0.9 copy-start.7
  9.8 0.7 copy-start.9
  10.5 0.7 copy-start.11
  11.2 0.7 copy-start.13
  105.5 2.1 %copy-start.14 = (f32[768,256]{1,0:T(8,128)S(1)}, f32[768,256]{1,0:T(8,128)}, u32[]{:S(2)}) copy-start(f32[768,256]{1,0:T(8,128)} %get-tuple-element.17) | copy-start | bytes 2359300

commit v2 on v1

--- a/solution.py
+++ b/solution.py
@@ -49,6 +49,30 @@
     fused,
     node_scale,
     edge_scale,
+    x_hbm,
+    agg_hbm,
+    ncot_hbm,
+    e_hbm,
+    ecot_hbm,
+    sloc_hbm,
+    rloc_hbm,
+    sslot_ref,
+    rslot_ref,
+    count_ref,
+    ewi_hbm,
+    ewo_hbm,
+    eg_hbm,
+    nwi_hbm,
+    nwo_hbm,
+    ng_hbm,
+    ngrad_ref,
+    egrad_ref,
+    egwi_out,
+    egwo_out,
+    ngwi_out,
+    ngwo_out,
+    egain_out,
+    ngain_out,
     x_ref,
     agg_ref,
     ncot_ref,
@@ -56,20 +80,15 @@
     ecot_ref,
     sloc_ref,
     rloc_ref,
-    sslot_ref,
-    rslot_ref,
-    count_ref,
     ewi_ref,
     ewo_ref,
     eg_ref,
     nwi_ref,
     nwo_ref,
     ng_ref,
-    ngrad_ref,
-    egrad_ref,
     egw_ref,
     ngw_ref,
-    gains_ref,
+    load_sem,
     req,
     req_in,
     onehot,
@@ -105,6 +124,25 @@
 ):
     nb, h = x_ref.shape
     edges = e_ref.shape[0]
+    loads = {}
+    for i, (name, src, dst) in enumerate(
+        (
+            ("sloc", sloc_hbm, sloc_ref),
+            ("rloc", rloc_hbm, rloc_ref),
+            ("x", x_hbm, x_ref),
+            ("nwi", nwi_hbm, nwi_ref),
+            ("agg", agg_hbm, agg_ref),
+            ("nwo", nwo_hbm, nwo_ref),
+            ("ng", ng_hbm, ng_ref),
+            ("ncot", ncot_hbm, ncot_ref),
+            ("e", e_hbm, e_ref),
+            ("ewi", ewi_hbm, ewi_ref),
+            ("ewo", ewo_hbm, ewo_ref),
+            ("eg", eg_hbm, eg_ref),
+            ("ecot", ecot_hbm, ecot_ref),
+        )
+    ):
+        loads[name] = pltpu.make_async_copy(src, dst, load_sem.at[i])
     tile = sloc_ref.shape[1]
     me = lax.axis_index("row")
     group = 4 * tile
@@ -130,6 +168,9 @@
     barrier = pltpu.get_barrier_semaphore()
     for p in partners:
         pl.semaphore_signal(barrier, inc=1, device_id={"row": p}, device_id_type=pl.DeviceIdType.MESH)
+
+    for c in loads.values():
+        c.start()
 
     used = [0]
 
@@ -147,6 +188,8 @@
         copy.start()
         return copy
 
+    loads["sloc"].wait()
+    loads["rloc"].wait()
     for side, (loc, slot) in enumerate(((sloc_ref, sslot_ref), (rloc_ref, rslot_ref))):
         tiles = [loc[j : j + 1, :] for j in range(6)]
         none = jnp.full((1, tile), -1, jnp.int32)
@@ -171,6 +214,7 @@
 
         lax.fori_loop(0, nb // 128, rows, 0)
 
+    loads["x"].wait()
     for k in (0, 3):
         make_onehot(k, req)
         lat_in[k] = mm_tn(onehot[k], x_ref[...]).astype(BF16)
@@ -182,6 +226,8 @@
         lats[k] = remote_copy(lat_out.at[k], lat_in.at[k], at(-hops[k]))
 
     gain_acc[...] = jnp.zeros_like(gain_acc)
+    for name in ("nwi", "agg", "nwo", "ng", "ncot"):
+        loads[name].wait()
 
     def node_rows(i, carry):
         r = pl.ds(pl.multiple_of(i * 256, 256), 256)
@@ -209,8 +255,14 @@
     def rows_of(lo, rows, part):
         return pl.ds(pl.multiple_of(lo + part * rows, 16), rows)
 
+    def give_weights(outs, rows):
+        split = outs[0].shape[0]
+        outs[0][...] = rows(0, split)
+        outs[1][...] = rows(split, split + h)
+
     class Sum:
-        def __init__(self, lo, total, scale, full):
+        def __init__(self, lo, total, scale, full, outs):
+            self.outs = outs
             self.lo, self.total, self.scale, self.full = lo, total, scale, full
             self.q = total // INNER
             self.e = self.q // outer
@@ -268,18 +320,20 @@
         def finish(self):
             for c in self.copies:
                 c.wait()
-            self.full[...] = w_fin[self.lo : self.lo + self.total, :].astype(F32)
+            give_weights(self.outs, lambda a, b: w_fin[self.lo + a : self.lo + b, :])
 
     n_total = ngw_ref.shape[0]
     e_total = egw_ref.shape[0]
-    edge_sum = Sum(0, e_total, edge_scale, egw_ref)
-    node_sum = Sum(e_total, n_total, node_scale, ngw_ref)
+    edge_sum = Sum(0, e_total, edge_scale, egw_ref, (egwi_out, egwo_out))
+    node_sum = Sum(e_total, n_total, node_scale, ngw_ref, (ngwi_out, ngwo_out))
     ngw_ref[0:h, :] = mm_tn(x_ref[...], n_dpre[...])
     ngw_ref[h : 2 * h, :] = mm_tn(agg_ref[...], n_dpre[...])
     ngw_ref[2 * h :, :] = mm_tn(n_act[...], n_dout[...])
     if fused:
         node_sum.start_a()
 
+    for name in ("e", "ewi", "ewo", "eg", "ecot"):
+        loads[name].wait()
     def unpack(side, slot, buffer, table):
         for j in range(6):
             lo = 0 if j < 3 else tile * (j - 2)
@@ -382,11 +436,14 @@
         g_sum = g_b[0]
         for i in range(1, outer):
             g_sum = g_sum + g_b[i]
-        gains_ref[0:8, :] = g_sum[0:8, :] * edge_scale
-        gains_ref[8:16, :] = g_sum[8:16, :] * node_scale
+        egain_out[...] = g_sum[0:1, :] * edge_scale
+        ngain_out[...] = g_sum[8:9, :] * node_scale
         edge_sum.finish()
     else:
-        gains_ref[...] = gain_acc[...]
+        egain_out[...] = gain_acc[0:1, :] * edge_scale
+        ngain_out[...] = gain_acc[8:9, :] * node_scale
+        give_weights(edge_sum.outs, lambda a, b: egw_ref[a:b, :] * edge_scale)
+        give_weights(node_sum.outs, lambda a, b: ngw_ref[a:b, :] * node_scale)
 
 
 def on_device(
@@ -422,18 +479,39 @@
     vmem = pl.BlockSpec(memory_space=pltpu.VMEM)
     smem = pl.BlockSpec(memory_space=pltpu.SMEM)
     copies = 14 + (2 * (2 * (INNER - 1) + 2 * (outer - 1)) + INNER - 1 + outer - 1 if fused else 0)
-    node_grad, edge_grad, egw, ngw, gains = pl.pallas_call(
+    anywhere = pl.BlockSpec(memory_space=pl.ANY)
+    summed = BF16 if fused else F32
+    node_grad, edge_grad, *sums = pl.pallas_call(
         functools.partial(layer_kernel, n, stride, fused, node_scale, edge_scale),
         out_shape=(
             jax.ShapeDtypeStruct((nb, h), BF16),
             jax.ShapeDtypeStruct((edges, h), BF16),
-            jax.ShapeDtypeStruct((4 * h, h), F32),
-            jax.ShapeDtypeStruct((3 * h, h), F32),
-            jax.ShapeDtypeStruct((16, h), F32),
+            jax.ShapeDtypeStruct((3 * h, h), summed),
+            jax.ShapeDtypeStruct((h, h), summed),
+            jax.ShapeDtypeStruct((2 * h, h), summed),
+            jax.ShapeDtypeStruct((h, h), summed),
+            jax.ShapeDtypeStruct((1, h), F32),
+            jax.ShapeDtypeStruct((1, h), F32),
         ),
-        in_specs=[vmem] * 7 + [smem] * 3 + [vmem] * 6,
-        out_specs=(vmem,) * 5,
+        in_specs=[anywhere] * 7 + [smem] * 3 + [anywhere] * 6,
+        out_specs=(vmem,) * 8,
         scratch_shapes=[
+            pltpu.VMEM((nb, h), BF16),
+            pltpu.VMEM((nb, h), BF16),
+            pltpu.VMEM((nb, h), BF16),
+            pltpu.VMEM((edges, h), BF16),
+            pltpu.VMEM((edges, h), BF16),
+            pltpu.VMEM((tile_total, tile), jnp.int32),
+            pltpu.VMEM((tile_total, tile), jnp.int32),
+            pltpu.VMEM((3 * h, h), BF16),
+            pltpu.VMEM((h, h), BF16),
+            pltpu.VMEM((1, h), F32),
+            pltpu.VMEM((2 * h, h), BF16),
+            pltpu.VMEM((h, h), BF16),
+            pltpu.VMEM((1, h), F32),
+            pltpu.VMEM((4 * h, h), F32),
+            pltpu.VMEM((3 * h, h), F32),
+            pltpu.SemaphoreType.DMA((13,)),
             pltpu.VMEM((6, 1, group), jnp.int32),
             pltpu.VMEM((6, 1, group), jnp.int32),
             pltpu.VMEM((6, nb, group), BF16),
@@ -468,7 +546,7 @@
             pltpu.SemaphoreType.DMA((copies,)),
         ],
         compiler_params=pltpu.CompilerParams(
-            collective_id=0, has_side_effects=True, vmem_limit_bytes=50 * 1024 * 1024
+            collective_id=0, has_side_effects=True, vmem_limit_bytes=60 * 1024 * 1024
         ),
         cost_estimate=pl.CostEstimate(flops=7 * 10**9, bytes_accessed=8 * 10**6, transcendentals=10**6),
     )(
@@ -490,18 +568,9 @@
         node_gain[None, :],
     )
     if not fused:
-        egw, ngw, gains = lax.psum((egw * edge_scale, ngw * node_scale, gains), "row")
-        gains = gains * jnp.repeat(jnp.array([edge_scale, node_scale], F32), 8)[:, None]
-    return (
-        node_grad,
-        edge_grad,
-        egw[: 3 * h],
-        egw[3 * h :],
-        gains[0],
-        ngw[: 2 * h],
-        ngw[2 * h :],
-        gains[8],
-    )
+        sums = lax.psum(tuple(sums), "row")
+    egwi, egwo, ngwi, ngwo, egain, ngain = [v.astype(F32) for v in sums]
+    return (node_grad, edge_grad, egwi, egwo, egain[0], ngwi, ngwo, ngain[0])
 
 
 def solution(mesh):

time: 112 us -> 101 us (0.902)
  local copies, waits for them, and re-layouts: 18 us -> 3.59 us
  other arithmetic: 0 us -> 4.24 us
    unnamed x32 -> x18, local copies, waits for them, and re-layouts: 12 us -> 3.59 us
    slice x5 -> x0, local copies, waits for them, and re-layouts: 5.92 us -> none  [the longest x1 2.14 us: on_device(): egw[:3 * h]]
    convert_element_type x0 -> x4, other arithmetic: none -> 4.24 us  [on_device(): egwi, egwo, ngwi, ngwo, egain, ngain = [v.astype(F32) for v in sums]]
where the time goes in v2:
time: 101 us
  Pallas kernels  91.4 us (90%)
  other arithmetic  4.24 us (4%)
  local copies, waits for them, and re-layouts  3.59 us (4%)
  between operations  1.31 us (1%)
    pallas_call x1, Pallas kernels, on_device(): pl.pallas_call(functools.partial(layer_kernel, n, stride, fused, node_sca...  91.4 us
    convert_element_type x4, other arithmetic, on_device(): egwi, egwo, ngwi, ngwo, egain, ngain = [v.astype(F32) for v in sums]  4.24 us
    unnamed x18, local copies, waits for them, and re-layouts  3.59 us

profile of v2, /device:TPU:0, one launch (start us, length us, event | category | flops | bytes accessed | tf_op | source)
XLA Modules:
  0.0 100.6 jit_solution(12501956593664657411)
XLA Ops:
  1.3 91.4 %shard_map.215 = (bf16[1024,256]{1,0:T(8,128)(2,1)}, bf16[768,256]{1,0:T(8,128)(2,1)}, bf16[768,256]{1,0:T(8,128)(2,1)}, bf16[256,256]{1,0:T(8,128)(2,1)}, bf16[...) custom-call(bf16[1024,256]{1,0:T(8,128)(2,1)} %x_hbm.1, ...), custom_call_target="tpu_custom_call" | custom-call | flops 7000000000 | bytes 8000000 | tf_op jit(solution)/shard_map/pallas_call | solution.py:484
  92.7 0.0 copy-start.4
  92.7 2.0 %convert_element_type.12 = f32[768,256]{1,0:T(8,128)} convert(bf16[768,256]{1,0:T(8,128)(2,1)} %get-tuple-element.18) | non-fusion elementwise | flops 196608 | bytes 1179648 | tf_op jit(solution)/shard_map/convert_element_type | solution.py:572
  94.7 0.0 copy-start.2
  94.7 0.0 copy-done.4
  94.7 0.7 convert_element_type.13
  95.4 0.3 copy-done.2
  95.7 0.0 copy-start.3
  95.7 0.0 copy-start
  95.8 0.8 convert_element_type.14
  96.6 0.1 copy-done.3
  96.7 0.7 convert_element_type.15
  97.4 0.0 copy-done
  97.4 0.0 copy-start.1
  97.4 0.8 copy.29
  98.2 0.4 copy-done.1
  98.6 0.0 copy-start.6
  98.6 0.7 copy.30
  99.3 0.0 copy-done.6
  99.3 0.0 copy-start.5
  99.3 0.6 copy.31
  99.9 0.1 copy-done.5
  100.0 0.6 copy.32
Async XLA Ops:
  92.7 2.0 %copy-start.4 = (bf16[256,256]{1,0:T(8,128)(2,1)S(1)}, bf16[256,256]{1,0:T(8,128)(2,1)}, u32[]{:S(2)}) copy-start(bf16[256,256]{1,0:T(8,128)(2,1)} %get-tuple-element.19) | copy-start | bytes 393220
  94.7 1.0 %copy-start.2 = (bf16[512,256]{1,0:T(8,128)(2,1)S(1)}, bf16[512,256]{1,0:T(8,128)(2,1)}, u32[]{:S(2)}) copy-start(bf16[512,256]{1,0:T(8,128)(2,1)} %get-tuple-element.21) | copy-start | bytes 786436
  95.7 0.9 copy-start.3
  95.7 1.6 %copy-start = (bf16[1024,256]{1,0:T(8,128)(2,1)S(1)}, bf16[1024,256]{1,0:T(8,128)(2,1)}, u32[]{:S(2)}) copy-start(bf16[1024,256]{1,0:T(8,128)(2,1)} %get-tuple-element.32) | copy-start | bytes 1572868
  97.4 1.2 %copy-start.1 = (bf16[768,256]{1,0:T(8,128)(2,1)S(1)}, bf16[768,256]{1,0:T(8,128)(2,1)}, u32[]{:S(2)}) copy-start(bf16[768,256]{1,0:T(8,128)(2,1)} %get-tuple-element.33) | copy-start | bytes 1179652
  98.6 0.8 copy-start.6
  99.3 0.7 copy-start.5

commit v3 on v2

--- a/solution.py
+++ b/solution.py
@@ -119,6 +119,7 @@
     w_fin,
     g_a,
     g_b,
+    hold,
     send_sem,
     recv_sem,
 ):
@@ -188,6 +189,62 @@
         copy.start()
         return copy
 
+    class Relayed:
+        def __init__(self, src, hold, dst, via, direct, first, second):
+            k = used[0]
+            used[0] += 3
+            self.src, self.hold, self.dst, self.k, self.via = src, hold, dst, k, via
+            self.direct, self.first, self.second = direct, first, second
+
+            @pl.when(via)
+            def _():
+                self.hop().start()
+
+            @pl.when(jnp.logical_not(via))
+            def _():
+                self.straight().start()
+
+        def make(self, src, dst, offset, send, recv):
+            return pltpu.make_async_remote_copy(
+                src_ref=src,
+                dst_ref=dst,
+                send_sem=send_sem.at[send],
+                recv_sem=recv_sem.at[recv],
+                device_id={"row": at(offset)},
+                device_id_type=pl.DeviceIdType.MESH,
+            )
+
+        def hop(self):
+            return self.make(self.src, self.hold, self.first, self.k, self.k)
+
+        def straight(self):
+            return self.make(self.src, self.dst, self.direct, self.k + 1, self.k + 1)
+
+        def onward(self):
+            return self.make(self.hold, self.dst, self.second, self.k + 2, self.k + 1)
+
+        def forward(self):
+            @pl.when(jnp.logical_not(self.via))
+            def _():
+                self.hop().wait_recv()
+                self.onward().start()
+
+        def wait(self):
+            self.straight().wait_recv()
+
+            @pl.when(self.via)
+            def _():
+                self.hop().wait_send()
+
+            @pl.when(jnp.logical_not(self.via))
+            def _():
+                self.straight().wait_send()
+                self.onward().wait_send()
+
+    relay = fused and stride == 2
+    x_low = lax.rem(me // 2, 2) == 0
+    x_high = jnp.logical_not(x_low)
+
     loads["sloc"].wait()
     loads["rloc"].wait()
     for side, (loc, slot) in enumerate(((sloc_ref, sslot_ref), (rloc_ref, rslot_ref))):
@@ -219,11 +276,14 @@
         make_onehot(k, req)
         lat_in[k] = mm_tn(onehot[k], x_ref[...]).astype(BF16)
     lats = {}
-    for k in (2, 5, 1, 4):
+    for k in (1, 2, 5, 4):
         asks[k].wait()
         make_onehot(k, req_in)
         lat_out[k] = mm_tn(onehot[k], x_ref[...]).astype(BF16)
-        lats[k] = remote_copy(lat_out.at[k], lat_in.at[k], at(-hops[k]))
+        if relay and k == 1:
+            lats[k] = Relayed(lat_out.at[k], hold.at[0], lat_in.at[k], x_low, -2, 2, -4)
+        else:
+            lats[k] = remote_copy(lat_out.at[k], lat_in.at[k], at(-hops[k]))
 
     gain_acc[...] = jnp.zeros_like(gain_acc)
     for name in ("nwi", "agg", "nwo", "ng", "ncot"):
@@ -246,10 +306,15 @@
         return carry
 
     lax.fori_loop(0, nb // 256, node_rows, 0)
+    if relay:
+        lats[1].forward()
     aggs = {}
     for s in (2, 1):
         agg_out[s] = mm_tn(onehot[3 + s], n_agg[...]).astype(BF16)
-        aggs[s] = remote_copy(agg_out.at[s], agg_in.at[s], at(-s))
+        if relay and s == 2:
+            aggs[s] = Relayed(agg_out.at[s], hold.at[1], agg_in.at[s], x_low, -2, 2, -4)
+        else:
+            aggs[s] = remote_copy(agg_out.at[s], agg_in.at[s], at(-s))
     agg_in[0] = mm_tn(onehot[3], n_agg[...]).astype(BF16)
 
     def rows_of(lo, rows, part):
@@ -343,6 +408,8 @@
     for k in (2, 1):
         lats[k].wait()
     unpack(0, sslot_ref, lat_in, snd)
+    if relay:
+        aggs[2].forward()
     for k in (5, 4):
         lats[k].wait()
     unpack(1, rslot_ref, lat_in, rcv)
@@ -386,7 +453,7 @@
     lax.fori_loop(0, edges // 256, edge_backward, 0)
 
     rets = {}
-    for k in (2, 5, 1, 4, 0, 3):
+    for k in (5, 1, 2, 4, 0, 3):
         s = k % 3
         grads, slot = (e_out, sslot_ref) if k < 3 else (e_pre, rslot_ref)
         target = ret_in if s == 0 else ret_out
@@ -394,7 +461,9 @@
         lead = lax.select(slot[0] == s, lead[0], lax.select(slot[1] == s, lead[1], lead[2]))
         target[k, 0:tile, :] = lead.astype(BF16)
         target[k, tile:, :] = grads[3 * tile :, :].astype(BF16)
-        if s:
+        if relay and k == 5:
+            rets[k] = Relayed(ret_out.at[k], hold.at[2], ret_in.at[k], x_high, 2, -2, 4)
+        elif s:
             rets[k] = remote_copy(ret_out.at[k], ret_in.at[k], at(hops[k]))
 
     if fused:
@@ -409,6 +478,8 @@
         gains = [remote_copy(gain_acc, g_a.at[ia], inner_peer(i)) for i in range(1, INNER)]
 
     n_base[...] += mm(onehot[0], ret_in[0]) + mm(onehot[3], ret_in[3])
+    if relay:
+        rets[5].forward()
     if fused:
         node_sum.finish()
         edge_sum.start_b()
@@ -478,7 +549,7 @@
     weights = 7 * h
     vmem = pl.BlockSpec(memory_space=pltpu.VMEM)
     smem = pl.BlockSpec(memory_space=pltpu.SMEM)
-    copies = 14 + (2 * (2 * (INNER - 1) + 2 * (outer - 1)) + INNER - 1 + outer - 1 if fused else 0)
+    copies = 20 + (2 * (2 * (INNER - 1) + 2 * (outer - 1)) + INNER - 1 + outer - 1 if fused else 0)
     anywhere = pl.BlockSpec(memory_space=pl.ANY)
     summed = BF16 if fused else F32
     node_grad, edge_grad, *sums = pl.pallas_call(
@@ -542,6 +613,7 @@
             pltpu.VMEM((weights, h), BF16),
             pltpu.VMEM((INNER, 16, h), F32),
             pltpu.VMEM((levels, 16, h), F32),
+            pltpu.VMEM((3, group, h), BF16),
             pltpu.SemaphoreType.DMA((copies,)),
             pltpu.SemaphoreType.DMA((copies,)),
         ],

time: 101 us -> 96 us (0.950)
  Pallas kernels: 91.4 us -> 86.5 us
    pallas_call x1, Pallas kernels: 91.4 us -> 86.5 us  [on_device(): pl.pallas_call(functools.partial(layer_kernel, n, stride, fused, node_sca...]
where the time goes in v3:
time: 96 us; the launch traced here: 95.7 us
  Pallas kernels  86.5 us (90%)
  other arithmetic  4.24 us (4%)
  local copies, waits for them, and re-layouts  3.59 us (4%)
  between operations  1.31 us (1%)
    pallas_call x1, Pallas kernels, on_device(): pl.pallas_call(functools.partial(layer_kernel, n, stride, fused, node_sca...  86.5 us
    convert_element_type x4, other arithmetic, on_device(): egwi, egwo, ngwi, ngwo, egain, ngain = [v.astype(F32) for v in sums]  4.24 us
    unnamed x18, local copies, waits for them, and re-layouts  3.59 us

profile of v3, /device:TPU:0, one launch (start us, length us, event | category | flops | bytes accessed | tf_op | source)
XLA Modules:
  0.0 95.7 jit_solution(2706436620748851833)
XLA Ops:
  1.3 86.5 %shard_map.215 = (bf16[1024,256]{1,0:T(8,128)(2,1)}, bf16[768,256]{1,0:T(8,128)(2,1)}, bf16[768,256]{1,0:T(8,128)(2,1)}, bf16[256,256]{1,0:T(8,128)(2,1)}, bf16[...) custom-call(bf16[1024,256]{1,0:T(8,128)(2,1)} %x_hbm.1, ...), custom_call_target="tpu_custom_call" | custom-call | flops 7000000000 | bytes 8000000 | tf_op jit(solution)/shard_map/pallas_call | solution.py:555
  87.8 0.0 copy-start.4
  87.8 2.0 %convert_element_type.12 = f32[768,256]{1,0:T(8,128)} convert(bf16[768,256]{1,0:T(8,128)(2,1)} %get-tuple-element.18) | non-fusion elementwise | flops 196608 | bytes 1179648 | tf_op jit(solution)/shard_map/convert_element_type | solution.py:644
  89.8 0.0 copy-start.2
  89.8 0.0 copy-done.4
  89.8 0.7 convert_element_type.13
  90.5 0.3 copy-done.2
  90.9 0.0 copy-start.3
  90.9 0.0 copy-start
  90.9 0.8 convert_element_type.14
  91.7 0.1 copy-done.3
  91.8 0.7 convert_element_type.15
  92.5 0.0 copy-done
  92.5 0.0 copy-start.1
  92.5 0.8 copy.29
  93.3 0.4 copy-done.1
  93.7 0.0 copy-start.6
  93.7 0.7 copy.30
  94.4 0.0 copy-done.6
  94.4 0.0 copy-start.5
  94.4 0.6 copy.31
  95.0 0.1 copy-done.5
  95.1 0.6 copy.32
Async XLA Ops:
  87.8 2.0 %copy-start.4 = (bf16[256,256]{1,0:T(8,128)(2,1)S(1)}, bf16[256,256]{1,0:T(8,128)(2,1)}, u32[]{:S(2)}) copy-start(bf16[256,256]{1,0:T(8,128)(2,1)} %get-tuple-element.19) | copy-start | bytes 393220
  89.8 1.0 %copy-start.2 = (bf16[512,256]{1,0:T(8,128)(2,1)S(1)}, bf16[512,256]{1,0:T(8,128)(2,1)}, u32[]{:S(2)}) copy-start(bf16[512,256]{1,0:T(8,128)(2,1)} %get-tuple-element.21) | copy-start | bytes 786436
  90.9 0.9 copy-start.3
  90.9 1.6 %copy-start = (bf16[1024,256]{1,0:T(8,128)(2,1)S(1)}, bf16[1024,256]{1,0:T(8,128)(2,1)}, u32[]{:S(2)}) copy-start(bf16[1024,256]{1,0:T(8,128)(2,1)} %get-tuple-element.32) | copy-start | bytes 1572868
  92.5 1.2 %copy-start.1 = (bf16[768,256]{1,0:T(8,128)(2,1)S(1)}, bf16[768,256]{1,0:T(8,128)(2,1)}, u32[]{:S(2)}) copy-start(bf16[768,256]{1,0:T(8,128)(2,1)} %get-tuple-element.33) | copy-start | bytes 1179652
  93.7 0.8 copy-start.6
  94.4 0.7 copy-start.5

commit v4 on v3

--- a/solution.py
+++ b/solution.py
@@ -431,6 +431,8 @@
     for s in (2, 1):
         aggs[s].wait()
     unpack(0, rslot_ref, agg_in, e_dpre)
+    if fused:
+        node_sum.start_d()
     live_rows = count_ref[0] * tile
 
     def edge_backward(i, carry):
@@ -452,6 +454,15 @@
 
     lax.fori_loop(0, edges // 256, edge_backward, 0)
 
+    egw_ref[0:h, :] = mm_tn(e_ref[...], e_dpre[...])
+    egw_ref[h : 2 * h, :] = mm_tn(snd[...], e_dpre[...])
+    egw_ref[2 * h : 3 * h, :] = mm_tn(rcv[...], e_dpre[...])
+    egw_ref[3 * h :, :] = mm_tn(e_act[...], e_dout[...])
+    if fused:
+        edge_sum.start_a()
+        g_a[ia] = gain_acc[...]
+        gains = [remote_copy(gain_acc, g_a.at[ia], inner_peer(i)) for i in range(1, INNER)]
+
     rets = {}
     for k in (5, 1, 2, 4, 0, 3):
         s = k % 3
@@ -466,22 +477,10 @@
         elif s:
             rets[k] = remote_copy(ret_out.at[k], ret_in.at[k], at(hops[k]))
 
-    if fused:
-        node_sum.start_d()
-    egw_ref[0:h, :] = mm_tn(e_ref[...], e_dpre[...])
-    egw_ref[h : 2 * h, :] = mm_tn(snd[...], e_dpre[...])
-    egw_ref[2 * h : 3 * h, :] = mm_tn(rcv[...], e_dpre[...])
-    egw_ref[3 * h :, :] = mm_tn(e_act[...], e_dout[...])
-    if fused:
-        edge_sum.start_a()
-        g_a[ia] = gain_acc[...]
-        gains = [remote_copy(gain_acc, g_a.at[ia], inner_peer(i)) for i in range(1, INNER)]
-
     n_base[...] += mm(onehot[0], ret_in[0]) + mm(onehot[3], ret_in[3])
     if relay:
         rets[5].forward()
     if fused:
-        node_sum.finish()
         edge_sum.start_b()
         for c in gains:
             c.wait()
@@ -497,6 +496,8 @@
     n_base[...] += mm(onehot[1], ret_in[1]) + mm(onehot[4], ret_in[4])
     if fused:
         edge_sum.start_d()
+    if fused:
+        node_sum.finish()
     for k in (2, 5):
         rets[k].wait()
     total = n_base[...] + mm(onehot[2], ret_in[2]) + mm(onehot[5], ret_in[5])

time: 96 us -> 102 us (1.062)
  Pallas kernels: 86.5 us -> 93 us
    pallas_call x1, Pallas kernels: 86.5 us -> 93 us  [on_device(): pl.pallas_call(functools.partial(layer_kernel, n, stride, fused, node_sca...]
where the time goes in v4:
time: 102 us
  Pallas kernels  93 us (91%)
  other arithmetic  4.24 us (4%)
  local copies, waits for them, and re-layouts  3.59 us (4%)
  between operations  1.31 us (1%)
    pallas_call x1, Pallas kernels, on_device(): pl.pallas_call(functools.partial(layer_kernel, n, stride, fused, node_sca...  93 us
    convert_element_type x4, other arithmetic, on_device(): egwi, egwo, ngwi, ngwo, egain, ngain = [v.astype(F32) for v in sums]  4.24 us
    unnamed x18, local copies, waits for them, and re-layouts  3.59 us

profile of v4, /device:TPU:0, one launch (start us, length us, event | category | flops | bytes accessed | tf_op | source)
XLA Modules:
  0.0 102.1 jit_solution(1345391927442237218)
XLA Ops:
  1.3 93.0 %shard_map.215 = (bf16[1024,256]{1,0:T(8,128)(2,1)}, bf16[768,256]{1,0:T(8,128)(2,1)}, bf16[768,256]{1,0:T(8,128)(2,1)}, bf16[256,256]{1,0:T(8,128)(2,1)}, bf16[...) custom-call(bf16[1024,256]{1,0:T(8,128)(2,1)} %x_hbm.1, ...), custom_call_target="tpu_custom_call" | custom-call | flops 7000000000 | bytes 8000000 | tf_op jit(solution)/shard_map/pallas_call | solution.py:556
  94.3 0.0 copy-start.4
  94.3 2.0 %convert_element_type.12 = f32[768,256]{1,0:T(8,128)} convert(bf16[768,256]{1,0:T(8,128)(2,1)} %get-tuple-element.18) | non-fusion elementwise | flops 196608 | bytes 1179648 | tf_op jit(solution)/shard_map/convert_element_type | solution.py:645
  96.3 0.0 copy-start.2
  96.3 0.0 copy-done.4
  96.3 0.7 convert_element_type.13
  97.0 0.3 copy-done.2
  97.3 0.0 copy-start.3
  97.3 0.0 copy-start
  97.3 0.8 convert_element_type.14
  98.1 0.1 copy-done.3
  98.2 0.7 convert_element_type.15
  99.0 0.0 copy-done
  99.0 0.0 copy-start.1
  99.0 0.8 copy.29
  99.8 0.4 copy-done.1
  100.1 0.0 copy-start.6
  100.1 0.7 copy.30
  100.9 0.0 copy-done.6
  100.9 0.0 copy-start.5
  100.9 0.6 copy.31
  101.5 0.1 copy-done.5
  101.6 0.6 copy.32
Async XLA Ops:
  94.3 2.0 %copy-start.4 = (bf16[256,256]{1,0:T(8,128)(2,1)S(1)}, bf16[256,256]{1,0:T(8,128)(2,1)}, u32[]{:S(2)}) copy-start(bf16[256,256]{1,0:T(8,128)(2,1)} %get-tuple-element.19) | copy-start | bytes 393220
  96.3 1.0 %copy-start.2 = (bf16[512,256]{1,0:T(8,128)(2,1)S(1)}, bf16[512,256]{1,0:T(8,128)(2,1)}, u32[]{:S(2)}) copy-start(bf16[512,256]{1,0:T(8,128)(2,1)} %get-tuple-element.21) | copy-start | bytes 786436
  97.3 0.9 copy-start.3
  97.3 1.6 %copy-start = (bf16[1024,256]{1,0:T(8,128)(2,1)S(1)}, bf16[1024,256]{1,0:T(8,128)(2,1)}, u32[]{:S(2)}) copy-start(bf16[1024,256]{1,0:T(8,128)(2,1)} %get-tuple-element.32) | copy-start | bytes 1572868
  99.0 1.2 %copy-start.1 = (bf16[768,256]{1,0:T(8,128)(2,1)S(1)}, bf16[768,256]{1,0:T(8,128)(2,1)}, u32[]{:S(2)}) copy-start(bf16[768,256]{1,0:T(8,128)(2,1)} %get-tuple-element.33) | copy-start | bytes 1179652
  100.1 0.8 copy-start.6
  100.9 0.7 copy-start.5
